TPU v7x, 32 devices: a whole 2x2x4 slice. The times are simulated.
32 devices in a mesh: tm: 16 (over z, y, core), space: 2 (over x).
Axes of the slice: x: 2, y: 2, z: 4, core: 2. Of those that a mesh axis runs over, the one named last changes fastest.
Arguments:
- start_states: float32 [16, 3, 4, 256, 256], P('tm', None, 'space'), may hold values from -6 to 6
- wall_normal: bfloat16 [256, 256], replicated, may hold values from -0.375 to 0.375
- spanwise: bfloat16 [256, 256], replicated, may hold values from -0.375 to 0.375
- base_flow: float32 [3, 256], replicated, may hold values from -1.5 to 1.5
Outputs:
- end_state: float32 [16, 3, 4, 256, 256], P('tm', None, 'space')
All inputs are finite; a program needn't handle non-finite values.
Results may differ from a plain program's by a relative error of at most 0.0017.
Values sent between devices are 32-bit elements; how exact they have to be, the bound alone decides.
A program may use at most 64 MiB of HBM per device.

v0:
```python
import jax
import jax.numpy as jnp
from jax import lax
from jax.sharding import PartitionSpec as P

TICKS = 2


step_size = 0.2


def padded_2(cells, sides, width):
    for axis, dim in sides:
        count = lax.axis_size(axis)
        head = lax.slice_in_dim(cells, 0, width, axis=dim)
        tail = lax.slice_in_dim(cells, cells.shape[dim] - width, cells.shape[dim], axis=dim)
        cells = jnp.concatenate(
            [
                lax.ppermute(tail, axis, [(i, (i + 1) % count) for i in range(count)]),
                cells,
                lax.ppermute(head, axis, [((i + 1) % count, i) for i in range(count)]),
            ],
            axis=dim,
        )
    return cells


def shifted(array, axis, by):
    length = lax.axis_size(axis)
    pairs = [(i, i + by) for i in range(length) if 0 <= i + by < length]
    return lax.ppermute(array, axis, pairs)


def tendency(padded, wall_normal, spanwise, base_flow):
    inner = padded[:, 1:-1]
    grad_x = 0.5 * (padded[:, 2:] - padded[:, :-2])
    rounded = inner.astype(jnp.bfloat16)
    grad_y = jnp.einsum("yk,cxkz->cxyz", wall_normal, rounded, preferred_element_type=jnp.float32)
    width = rounded.shape[-1]
    grad_z = jnp.dot(
        rounded.reshape(-1, width), spanwise, preferred_element_type=jnp.float32
    ).reshape(inner.shape)
    velocity = base_flow[:, None, :, None] + inner
    return -(velocity[0:1] * grad_x + velocity[1:2] * grad_y + velocity[2:3] * grad_z)


def local(start_states, wall_normal, spanwise, base_flow):
    begin = start_states[0]
    leading = lax.axis_index("tm") == 0
    begin_wide = padded_2(begin, (("space", 1),), 1)
    finish = begin
    finish_wide = begin_wide
    old_rate = tendency(begin_wide, wall_normal, spanwise, base_flow)
    fresh = old_rate
    for tick in range(TICKS):
        final = tick == TICKS - 1
        end_rate = tendency(finish_wide, wall_normal, spanwise, base_flow)
        if tick > 0:
            passed = shifted(end_rate, "tm", 1)
            fresh = jnp.where(leading, fresh, passed)
        finish = begin + step_size * (fresh - old_rate) + 0.5 * step_size * (old_rate + end_rate)
        old_rate = fresh
        if not final:
            moved = shifted(finish, "tm", 1)
            begin = jnp.where(leading, begin, moved)
            finish_wide = padded_2(finish, (("space", 1),), 1)
    return finish[None]


def solution(mesh):
    placed = (P("tm", None, "space", None, None), P(), P(), P())
    return jax.shard_map(
        local,
        mesh=mesh,
        in_specs=placed,
        out_specs=P("tm", None, "space", None, None),
        check_vma=False,
    )
```

profile of v0, /device:TPU:24, one launch (start us, length us, event | category | flops | bytes accessed | tf_op | source)
XLA Modules:
  0.0 106.0 jit_solution(18080243163962051364)
XLA Ops:
  0.0 0.0 copy-start
  0.0 1.9 %copy.5 = f32[1,3,2,256,256]{3,4,2,1,0:T(8,128)S(1)} copy(f32[1,3,2,256,256]{4,3,2,1,0:T(8,128)} %param.4) | data formatting | bytes 3145728 | tf_op args[0]
  1.9 0.0 copy-start.2
  1.9 0.1 fusion.29
  2.0 1.6 %collective-permute-start = (f32[3,1,256,256]{2,3,1,0:T(8,128)S(1)}, f32[3,1,256,256]{2,3,1,0:T(8,128)S(1)}, u32[]{:S(2)}, u32[]{:S(2)}) collective-permute-start(f32[3,1,256,256]{2,3,1,0:T(8,128)S(1)} %get-tuple-element.15), channel_id=1, source_target_pairs={{1,0},{0,1},{3,2},{2,3},{5,4},{4,5},{7,6},{6,7},{9,8},{8,9},{11,10... | collective-permute-start | bytes 2359304 | tf_op jit(solution)/shard_map/ppermute | solution.py:21
  3.6 0.5 collective-permute-start.1
  4.1 0.0 copy-done.2
  4.1 0.2 broadcast_add_fusion.1
  4.3 0.0 copy-start.1
  4.3 0.2 fusion.15
  4.5 0.7 copy-done.1
  5.2 0.4 fusion.19
  5.6 16.9 %collective-permute-done = f32[3,1,256,256]{2,3,1,0:T(8,128)S(1)} collective-permute-done((f32[3,1,256,256]{2,3,1,0:T(8,128)S(1)}, f32[3,1,256,256]{2,3,1,0:T(8,128)S(1)}, u32[]{:S(2)}, u32[]{:S(2)}) %collective-permute-start) | collective-permute-done | bytes 786464 | tf_op jit(solution)/shard_map/ppermute | solution.py:21
  22.5 15.7 %collective-permute-done.1 = f32[3,1,256,256]{2,3,1,0:T(8,128)S(1)} collective-permute-done((f32[3,1,256,256]{2,3,1,0:T(8,128)S(1)}, f32[3,1,256,256]{2,3,1,0:T(8,128)S(1)}, u32[]{:S(2)}, u32[]{:S(2)}) %collective-permute-start.1) | collective-permute-done | bytes 786464 | tf_op jit(solution)/shard_map/ppermute | solution.py:19
  38.2 0.0 copy-done
  38.2 2.2 %broadcast_add_fusion = (f32[3,2,256,256]{2,3,1,0:T(8,128)S(1)}, f32[3,2,256,256]{2,3,1,0:T(8,128)S(1)}, f32[3,2,256,256]{2,3,1,0:T(8,128)}) fusion(f32[3,256]{1,0:T(4,128)S(1)} %copy-done.2, f32[1,3,2,256,256]{3,4,2,1,0:T(8,128)S(1)} %copy.5, f32[3,2,256,256]{2,3,1,0:T(8,128)S(1)} %fusion.19, f32[2,256,256]{1,2,0:T(8,128)S(1)} %get-tuple-element.13, ...), kind=kOutput, calls=%fused_computation.22 | convolution fusion | flops 208011264 | bytes 12717056 | tf_op jit(solution)/shard_map/yk,cxkz->cxyz/dot_general | solution.py:38
  40.4 0.1 fusion.28
  40.5 1.6 %collective-permute-start.3 = (f32[3,1,256,256]{2,3,1,0:T(8,128)S(1)}, f32[3,1,256,256]{2,3,1,0:T(8,128)S(1)}, u32[]{:S(2)}, u32[]{:S(2)}) collective-permute-start(f32[3,1,256,256]{2,3,1,0:T(8,128)S(1)} %get-tuple-element.10), channel_id=1, source_target_pairs={{1,0},{0,1},{3,2},{2,3},{5,4},{4,5},{7,6},{6,7},{9,8},{8,9},{11,10... | collective-permute-start | bytes 2359304 | tf_op jit(solution)/shard_map/ppermute | solution.py:21
  42.1 0.5 collective-permute-start.4
  42.6 1.9 %collective-permute-start.2 = (f32[3,2,256,256]{2,3,1,0:T(8,128)S(1)}, f32[3,2,256,256]{2,3,1,0:T(8,128)}, u32[]{:S(2)}, u32[]{:S(2)}) collective-permute-start(f32[3,2,256,256]{2,3,1,0:T(8,128)S(1)} %get-tuple-element.6), channel_id=1, source_target_pairs={{0,2},{2,4},{4,6},{6,8},{8,10},{10,12},{12,14},{14,16},{16,18},{18... | collective-permute-start | bytes 4718600 | tf_op jit(solution)/shard_map/ppermute | solution.py:31
  44.5 0.1 fusion.14
  44.6 0.4 fusion.16
  45.1 16.0 %collective-permute-done.3 = f32[3,1,256,256]{2,3,1,0:T(8,128)S(1)} collective-permute-done((f32[3,1,256,256]{2,3,1,0:T(8,128)S(1)}, f32[3,1,256,256]{2,3,1,0:T(8,128)S(1)}, u32[]{:S(2)}, u32[]{:S(2)}) %collective-permute-start.3) | collective-permute-done | bytes 786464 | tf_op jit(solution)/shard_map/ppermute | solution.py:21
  61.1 14.8 %collective-permute-done.4 = f32[3,1,256,256]{2,3,1,0:T(8,128)S(1)} collective-permute-done((f32[3,1,256,256]{2,3,1,0:T(8,128)S(1)}, f32[3,1,256,256]{2,3,1,0:T(8,128)S(1)}, u32[]{:S(2)}, u32[]{:S(2)}) %collective-permute-start.4) | collective-permute-done | bytes 786464 | tf_op jit(solution)/shard_map/ppermute | solution.py:19
  75.8 2.2 %fusion.8 = f32[3,2,256,256]{2,3,1,0:T(8,128)} fusion(f32[3,2,256,256]{2,3,1,0:T(8,128)S(1)} %get-tuple-element.6, f32[3,1,256,256]{2,3,1,0:T(8,128)S(1)} %collective-permute-done.4, f32[3,1,256,256]{2,3,1,0:T(8,128)S(1)} %collective-permute-done.3, f32[3,2,256,256]{2,3,1,0:T(8,128)S(1)} %fusion.16, f32[2,256,256]{1,2,0:T(8,128)S(1)} %get-tuple-element.8, ...), kind=kOutput, calls=%fused_computation.10 | convolution fusion | flops 205258752 | bytes 7995392 | tf_op jit(solution)/shard_map/yk,cxkz->cxyz/dot_general | solution.py:38
  78.0 1.9 %collective-permute-start.5 = (f32[3,2,256,256]{2,3,1,0:T(8,128)}, f32[3,2,256,256]{2,3,1,0:T(8,128)}, u32[]{:S(2)}, u32[]{:S(2)}) collective-permute-start(f32[3,2,256,256]{2,3,1,0:T(8,128)} %fusion.8), channel_id=1, source_target_pairs={{0,2},{2,4},{4,6},{6,8},{8,10},{10,12},{12,14},{14,16},{16,18},{18... | collective-permute-start | bytes 4718600 | tf_op jit(solution)/shard_map/ppermute | solution.py:31
  80.0 0.0 collective-permute-done.2
  80.0 21.0 %collective-permute-done.5 = f32[3,2,256,256]{2,3,1,0:T(8,128)} collective-permute-done((f32[3,2,256,256]{2,3,1,0:T(8,128)}, f32[3,2,256,256]{2,3,1,0:T(8,128)}, u32[]{:S(2)}, u32[]{:S(2)}) %collective-permute-start.5) | collective-permute-done | bytes 1572896 | tf_op jit(solution)/shard_map/ppermute | solution.py:31
  101.0 3.4 %fusion.3 = f32[1,3,2,256,256]{3,4,2,1,0:T(8,128)S(1)} fusion(f32[3,2,256,256]{2,3,1,0:T(8,128)} %get-tuple-element.17, f32[3,2,256,256]{2,3,1,0:T(8,128)} %collective-permute-done.5, f32[3,2,256,256]{2,3,1,0:T(8,128)} %fusion.8, f32[3,2,256,256]{2,3,1,0:T(8,128)} %collective-permute-done.2, pred[]{:T(512)S(6)} %eq.3, f32[1,3,2,256,256]{3,4,2,1,0:T(8,128)S(1)} %copy.5), kind=kLoop, calls=%fused_computation.4 | loop fusion | flops 3145728 | bytes 9437185 | tf_op jit(solution)/shard_map/broadcast_in_dim | solution.py:67
  104.3 1.6 %copy.10 = f32[1,3,2,256,256]{4,3,2,1,0:T(8,128)} copy(f32[1,3,2,256,256]{3,4,2,1,0:T(8,128)S(1)} %fusion.3) | data formatting | bytes 3145728 | tf_op jit(solution)/shard_map/broadcast_in_dim | solution.py:67
Async XLA Ops:
  0.0 38.2 %copy-start = (bf16[256,256]{1,0:T(8,128)(2,1)S(1)}, bf16[256,256]{1,0:T(8,128)(2,1)}, u32[]{:S(2)}) copy-start(bf16[256,256]{1,0:T(8,128)(2,1)} %param.5) | copy-start | bytes 393220
  1.9 2.2 %copy-start.2 = (f32[3,256]{1,0:T(4,128)S(1)}, f32[3,256]{1,0:T(4,128)}, u32[]{:S(2)}) copy-start(f32[3,256]{1,0:T(4,128)} %param.7) | copy-start | bytes 9220
  2.0 20.5 %collective-permute-start = (f32[3,1,256,256]{2,3,1,0:T(8,128)S(1)}, f32[3,1,256,256]{2,3,1,0:T(8,128)S(1)}, u32[]{:S(2)}, u32[]{:S(2)}) collective-permute-start(f32[3,1,256,256]{2,3,1,0:T(8,128)S(1)} %get-tuple-element.15), channel_id=1, source_target_pairs={{1,0},{0,1},{3,2},{2,3},{5,4},{4,5},{7,6},{6,7},{9,8},{8,9},{11,10... | collective-permute-start | bytes 2359304 | tf_op jit(solution)/shard_map/ppermute | solution.py:21
  3.6 34.6 %collective-permute-start.1 = (f32[3,1,256,256]{2,3,1,0:T(8,128)S(1)}, f32[3,1,256,256]{2,3,1,0:T(8,128)S(1)}, u32[]{:S(2)}, u32[]{:S(2)}) collective-permute-start(f32[3,1,256,256]{2,3,1,0:T(8,128)S(1)} %get-tuple-element.16), channel_id=1, source_target_pairs={{0,1},{1,0},{2,3},{3,2},{4,5},{5,4},{6,7},{7,6},{8,9},{9,8},{10,11... | collective-permute-start | bytes 2359304 | tf_op jit(solution)/shard_map/ppermute | solution.py:19
  4.3 0.9 copy-start.1
  40.5 20.5 %collective-permute-start.3 = (f32[3,1,256,256]{2,3,1,0:T(8,128)S(1)}, f32[3,1,256,256]{2,3,1,0:T(8,128)S(1)}, u32[]{:S(2)}, u32[]{:S(2)}) collective-permute-start(f32[3,1,256,256]{2,3,1,0:T(8,128)S(1)} %get-tuple-element.10), channel_id=1, source_target_pairs={{1,0},{0,1},{3,2},{2,3},{5,4},{4,5},{7,6},{6,7},{9,8},{8,9},{11,10... | collective-permute-start | bytes 2359304 | tf_op jit(solution)/shard_map/ppermute | solution.py:21
  42.1 33.8 %collective-permute-start.4 = (f32[3,1,256,256]{2,3,1,0:T(8,128)S(1)}, f32[3,1,256,256]{2,3,1,0:T(8,128)S(1)}, u32[]{:S(2)}, u32[]{:S(2)}) collective-permute-start(f32[3,1,256,256]{2,3,1,0:T(8,128)S(1)} %get-tuple-element.11), channel_id=1, source_target_pairs={{0,1},{1,0},{2,3},{3,2},{4,5},{5,4},{6,7},{7,6},{8,9},{9,8},{10,11... | collective-permute-start | bytes 2359304 | tf_op jit(solution)/shard_map/ppermute | solution.py:19
  42.6 37.4 %collective-permute-start.2 = (f32[3,2,256,256]{2,3,1,0:T(8,128)S(1)}, f32[3,2,256,256]{2,3,1,0:T(8,128)}, u32[]{:S(2)}, u32[]{:S(2)}) collective-permute-start(f32[3,2,256,256]{2,3,1,0:T(8,128)S(1)} %get-tuple-element.6), channel_id=1, source_target_pairs={{0,2},{2,4},{4,6},{6,8},{8,10},{10,12},{12,14},{14,16},{16,18},{18... | collective-permute-start | bytes 4718600 | tf_op jit(solution)/shard_map/ppermute | solution.py:31
  78.0 22.9 %collective-permute-start.5 = (f32[3,2,256,256]{2,3,1,0:T(8,128)}, f32[3,2,256,256]{2,3,1,0:T(8,128)}, u32[]{:S(2)}, u32[]{:S(2)}) collective-permute-start(f32[3,2,256,256]{2,3,1,0:T(8,128)} %fusion.8), channel_id=1, source_target_pairs={{0,2},{2,4},{4,6},{6,8},{8,10},{10,12},{12,14},{14,16},{16,18},{18... | collective-permute-start | bytes 4718600 | tf_op jit(solution)/shard_map/ppermute | solution.py:31
where the time goes:
time: 106 us
  waiting for transfers between devices  84.4 us (80%)
  starting transfers between devices  8 us (8%)
  matrix products  5.18 us (5%)
  local copies, waits for them, and re-layouts  4.46 us (4%)
  other arithmetic  3.82 us (4%)
    ppermute x2, waiting for transfers between devices, padded_2(): lax.ppermute(head, axis, [((i + 1) % count, i) for i in range(count)])  32.9 us
    ppermute x2, waiting for transfers between devices, padded_2(): lax.ppermute(tail, axis, [(i, (i + 1) % count) for i in range(count)])  30.5 us
    ppermute x2, waiting for transfers between devices, shifted(): return lax.ppermute(array, axis, pairs)  21 us
    dot_general x2, matrix products, tendency(): jnp.einsum('yk,cxkz->cxyz', wall_normal, rounded, preferred_element_type=...  4.36 us
    ppermute x2, starting transfers between devices, shifted(): return lax.ppermute(array, axis, pairs)  3.82 us
    broadcast_in_dim x1, other arithmetic, local(): return finish[None]  3.36 us
    ppermute x2, starting transfers between devices, padded_2(): lax.ppermute(head, axis, [((i + 1) % count, i) for i in range(count)])  3.11 us
    unnamed x7, local copies, waits for them, and re-layouts  2.64 us
  transfers between devices with their start and end apart: 6, of which 5 were waited for; matrix products, arithmetic and copies ran while one was open for 3% of the time, Pallas kernels for 0%

commit v1 on v0

v1 whole, which is shorter than its diff:
```python
import functools

import jax
import jax.numpy as jnp
from jax import lax
from jax.experimental import pallas as pl
from jax.experimental.pallas import tpu as pltpu
from jax.sharding import PartitionSpec as P

MESH = pl.DeviceIdType.MESH
ROWS = 32
STEP = 0.2


def layout(count, planes):
    if count == 2 and planes == 2:
        sends = [(0, 0, 1), (1, 1, 1)]
        return sends, 2, lambda e: e + 2 if e < 0 else e - planes
    sends = [(planes - 2, 0, 1), (planes - 1, 1, 1), (0, 2, -1), (1, 3, -1)]
    return sends, 4, lambda e: e + 2 if e < 0 else e - planes + 2


def kernel(ticks_axis, count, start, wall, span, base, out, own, far, gy, gz, u1, gyr, gzr, u1r,
           rate, ub, load_sem, xs, xr, ts, tr, fs, fr):
    comps, planes, height, width = start.shape[1:]
    sends, slots, slot = layout(count, planes)
    t = lax.axis_index("tm")
    x = lax.axis_index("space")
    right, left = lax.rem(x + 1, count), lax.rem(x + count - 1, count)
    has_prev, has_next = t > 0, t < ticks_axis - 1

    load = pltpu.make_async_copy(start.at[0], own.at[0], load_sem)
    load.start()

    barrier = pltpu.get_barrier_semaphore()
    sides = [right] if slots == 2 else [right, left]
    for side in sides:
        pl.semaphore_signal(barrier, inc=1, device_id={"space": side}, device_id_type=MESH)

    @pl.when(has_prev)
    def _():
        pl.semaphore_signal(barrier, inc=1, device_id={"tm": t - 1}, device_id_type=MESH)

    @pl.when(has_next)
    def _():
        pl.semaphore_signal(barrier, inc=1, device_id={"tm": t + 1}, device_id_type=MESH)

    pl.semaphore_wait(barrier, len(sides) + has_prev.astype(jnp.int32) + has_next.astype(jnp.int32))

    def across(c, i):
        p, k, way = sends[i]
        return pltpu.make_async_remote_copy(
            src_ref=start.at[0, c, p], dst_ref=far.at[0, c, k], send_sem=xs.at[c, k], recv_sem=xr.at[c, k],
            device_id={"space": right if way == 1 else left}, device_id_type=MESH)

    def onward(c):
        return pltpu.make_async_remote_copy(
            src_ref=start.at[0, c], dst_ref=own.at[1, c], send_sem=ts.at[c], recv_sem=tr.at[c],
            device_id={"tm": t + 1}, device_id_type=MESH)

    def forward(c, k):
        return pltpu.make_async_remote_copy(
            src_ref=far.at[0, c, k], dst_ref=far.at[1, c, k], send_sem=fs.at[c, k], recv_sem=fr.at[c, k],
            device_id={"tm": t + 1}, device_id_type=MESH)

    for c in range(comps):
        for i in range(len(sends)):
            across(c, i).start()

    @pl.when(has_next)
    def _():
        for c in range(comps):
            onward(c).start()

    for c in range(comps):
        ub[c] = jnp.broadcast_to(base[c][None, :], (width, height)).T

    def grads(src, to_y, to_z):
        rounded = src[...].astype(jnp.bfloat16)
        to_y[...] = jnp.dot(wall[...], rounded, preferred_element_type=jnp.float32)
        to_z[...] = jnp.dot(rounded, span[...], preferred_element_type=jnp.float32)

    def plane(g, c, e):
        return own.at[g, c, e] if 0 <= e < planes else far.at[g, c, slot(e)]

    def after(g, c, e):
        return u1.at[g, c, e] if 0 <= e < planes else u1r.at[g, c, 0 if e < 0 else 1]

    def blocks(body):
        @pl.loop(0, height // ROWS)
        def _(b):
            body(pl.ds(pl.multiple_of(b * ROWS, ROWS), ROWS))

    def first(g):
        for c in range(comps):
            for p in range(planes):
                grads(own.at[g, c, p], gy.at[g, c, p], gz.at[g, c, p])

    def second(g, c):
        for i, e in enumerate((-1, planes)):
            grads(plane(g, c, e), gyr.at[g, c, i], gzr.at[g, c, i])
        for p in range(planes):
            def body(r):
                gx = 0.5 * (plane(g, c, p + 1)[r] - plane(g, c, p - 1)[r])
                f = -((ub[0, r] + own[g, 0, p, r]) * gx + (ub[1, r] + own[g, 1, p, r]) * gy[g, c, p, r]
                      + (ub[2, r] + own[g, 2, p, r]) * gz[g, c, p, r])
                if g == 0:
                    rate[c, p, r] = f
                u1[g, c, p, r] = own[g, c, p, r] + STEP * f
            blocks(body)
            grads(u1.at[g, c, p], gy.at[g, c, p], gz.at[g, c, p])

    def third(g):
        for i, e in enumerate((-1, planes)):
            def body(r):
                v = [ub[d, r] + plane(g, d, e)[r] for d in range(3)]
                for c in range(comps):
                    gx = 0.5 * (plane(g, c, e + 1)[r] - plane(g, c, e - 1)[r])
                    f = -(v[0] * gx + v[1] * gyr[g, c, i, r] + v[2] * gzr[g, c, i, r])
                    u1r[g, c, i, r] = plane(g, c, e)[r] + STEP * f
            blocks(body)

    def fourth(g, finish):
        for p in range(planes):
            def body(r):
                v = [ub[d, r] + u1[g, d, p, r] for d in range(3)]
                for c in range(comps):
                    gx = 0.5 * (after(g, c, p + 1)[r] - after(g, c, p - 1)[r])
                    finish(c, p, r, -(v[0] * gx + v[1] * gy[g, c, p, r] + v[2] * gz[g, c, p, r]))
            blocks(body)

    def own_part(c, p, r, f):
        rate[c, p, r] = 0.5 * STEP * (f - rate[c, p, r])

    def alone(c, p, r, f):
        out[0, c, p, r] = u1[0, c, p, r] + 0.5 * STEP * (f - rate[c, p, r])

    def joined(c, p, r, f):
        out[0, c, p, r] = u1[1, c, p, r] + STEP * f + rate[c, p, r]

    def arrive(c):
        for _, k, _ in sends:
            i = [s[1] for s in sends].index(k)
            across(c, i).wait_recv()

            @pl.when(has_next)
            def _():
                forward(c, k).start()

    def prev_arrive(c):
        for _, k, _ in sends:
            forward(c, k).wait_recv()

    load.wait()
    first(0)
    arrive(0)
    second(0, 0)
    arrive(1)
    second(0, 1)

    @pl.when(has_prev)
    def _():
        for c in range(comps):
            onward(c).wait_recv()
        first(1)
        prev_arrive(0)
        second(1, 0)

    arrive(2)
    second(0, 2)
    third(0)

    @pl.when(t == 0)
    def _():
        fourth(0, alone)

    @pl.when(has_prev)
    def _():
        fourth(0, own_part)
        for c in range(1, comps):
            prev_arrive(c)
            second(1, c)
        third(1)
        fourth(1, joined)

    for c in range(comps):
        for i in range(len(sends)):
            across(c, i).wait_send()

    @pl.when(has_next)
    def _():
        for c in range(comps):
            onward(c).wait_send()
            for _, k, _ in sends:
                forward(c, k).wait_send()


def local(ticks_axis, count, start_states, wall_normal, spanwise, base_flow):
    _, comps, planes, height, width = start_states.shape
    slots = layout(count, planes)[1]
    vmem = lambda *shape: pltpu.VMEM(shape, jnp.float32)
    state = lambda *lead: vmem(*lead, height, width)
    return pl.pallas_call(
        functools.partial(kernel, ticks_axis, count),
        out_shape=jax.ShapeDtypeStruct(start_states.shape, jnp.float32),
        in_specs=[pl.BlockSpec(memory_space=pl.ANY)] + [pl.BlockSpec(memory_space=pltpu.VMEM)] * 3,
        out_specs=pl.BlockSpec(memory_space=pltpu.VMEM),
        scratch_shapes=[
            state(2, comps, planes), state(2, comps, slots),
            state(2, comps, planes), state(2, comps, planes), state(2, comps, planes),
            state(2, comps, 2), state(2, comps, 2), state(2, comps, 2),
            state(comps, planes), state(3),
            pltpu.SemaphoreType.DMA,
            pltpu.SemaphoreType.DMA((comps, slots)), pltpu.SemaphoreType.DMA((comps, slots)),
            pltpu.SemaphoreType.DMA((comps,)), pltpu.SemaphoreType.DMA((comps,)),
            pltpu.SemaphoreType.DMA((comps, slots)), pltpu.SemaphoreType.DMA((comps, slots)),
        ],
        compiler_params=pltpu.CompilerParams(
            collective_id=0, has_side_effects=True, vmem_limit_bytes=50 * 1024 * 1024),
    )(start_states, wall_normal, spanwise, base_flow)


def solution(mesh):
    return jax.shard_map(
        functools.partial(local, mesh.shape["tm"], mesh.shape["space"]),
        mesh=mesh,
        in_specs=(P("tm", None, "space", None, None), P(), P(), P()),
        out_specs=P("tm", None, "space", None, None),
        check_vma=False,
    )
```

time: 106 us -> 50.5 us (0.48)
  waiting for transfers between devices: 84.4 us -> 0 us
  Pallas kernels: 0 us -> 45.3 us
  starting transfers between devices: 8 us -> 0 us
  matrix products: 5.18 us -> 0 us
  other arithmetic: 3.82 us -> 0 us
    ppermute x6 -> x0, waiting for transfers between devices: 84.4 us -> none  [the longest x2 32.9 us: padded_2(): lax.ppermute(head, axis, [((i + 1) % count, i) for i in range(count)])]
    pallas_call x0 -> x1, Pallas kernels: none -> 45.3 us  [local(): pl.pallas_call(functools.partial(kernel, ticks_axis, count), out_shape=ja...]
    ppermute x6 -> x0, starting transfers between devices: 8 us -> none  [the longest x2 3.82 us: shifted(): return lax.ppermute(array, axis, pairs)]
    dot_general x4 -> x0, matrix products: 5.18 us -> none  [the longest x2 4.36 us: tendency(): jnp.einsum('yk,cxkz->cxyz', wall_normal, rounded, preferred_element_type=...]
    broadcast_in_dim x1 -> x0, other arithmetic: 3.36 us -> none  [local(): return finish[None]]
    unnamed x7 -> x9, local copies, waits for them, and re-layouts: 2.64 us -> 5.05 us
    broadcast_in_dim x1 -> x0, local copies, waits for them, and re-layouts: 1.61 us -> none  [local(): return finish[None]]
  transfers between devices with their start and end apart: 6 -> 0, of which waited for: 5 -> 0; matrix products, arithmetic and copies ran while one was open for 3% -> 0% of each run, Pallas kernels for 0% -> 0%
where the time goes in v1:
time: 50.5 us; the launch traced here: 50.3 us
  Pallas kernels  45.3 us (90%)
  local copies, waits for them, and re-layouts  5.05 us (10%)
    pallas_call x1, Pallas kernels, local(): pl.pallas_call(functools.partial(kernel, ticks_axis, count), out_shape=ja...  45.3 us
    unnamed x9, local copies, waits for them, and re-layouts  5.05 us

profile of v1, /device:TPU:24, one launch (start us, length us, event | category | flops | bytes accessed | tf_op | source)
XLA Modules:
  0.0 50.3 jit_solution(8020627086160674370)
XLA Ops:
  0.0 0.0 copy-start
  0.0 1.4 %copy-done = f32[1,3,2,256,256]{4,3,2,1,0:T(8,128)S(1)} copy-done((f32[1,3,2,256,256]{4,3,2,1,0:T(8,128)S(1)}, f32[1,3,2,256,256]{4,3,2,1,0:T(8,128)}, u32[]{:S(2)}) %copy-start) | copy-done | bytes 1572888
  1.4 0.0 copy-start.1
  1.4 0.9 %copy-done.1 = bf16[256,256]{1,0:T(8,128)(2,1)S(1)} copy-done((bf16[256,256]{1,0:T(8,128)(2,1)S(1)}, bf16[256,256]{1,0:T(8,128)(2,1)}, u32[]{:S(2)}) %copy-start.1) | copy-done | bytes 131096
  2.3 0.0 copy-start.2
  2.3 0.9 %copy-done.2 = bf16[256,256]{1,0:T(8,128)(2,1)S(1)} copy-done((bf16[256,256]{1,0:T(8,128)(2,1)S(1)}, bf16[256,256]{1,0:T(8,128)(2,1)}, u32[]{:S(2)}) %copy-start.2) | copy-done | bytes 131096
  3.2 0.0 copy-start.3
  3.2 0.7 %copy-done.3 = f32[3,256]{1,0:T(4,128)S(1)} copy-done((f32[3,256]{1,0:T(4,128)S(1)}, f32[3,256]{1,0:T(4,128)}, u32[]{:S(2)}) %copy-start.3) | copy-done | bytes 3096
  3.9 45.3 %shard_map.46 = f32[1,3,2,256,256]{4,3,2,1,0:T(8,128)S(1)} custom-call(f32[1,3,2,256,256]{4,3,2,1,0:T(8,128)S(1)} %copy-done, bf16[256,256]{1,0:T(8,128)(2,1)S(1)} %copy-done.1, bf16[256,256]{1,0:T(8,128)(2,1)S(1)} %copy-done.2, f32[3,256]{1,0:T(4,128)S(1)} %copy-done.3), custom_call_target="tpu_custom_call" | custom-call | tf_op jit(solution)/shard_map/pallas_call | solution.py:203
  49.2 1.1 %copy.6 = f32[1,3,2,256,256]{4,3,2,1,0:T(8,128)} copy(f32[1,3,2,256,256]{4,3,2,1,0:T(8,128)S(1)} %shard_map.46) | data formatting | bytes 3145728
Async XLA Ops:
  0.0 1.4 %copy-start = (f32[1,3,2,256,256]{4,3,2,1,0:T(8,128)S(1)}, f32[1,3,2,256,256]{4,3,2,1,0:T(8,128)}, u32[]{:S(2)}) copy-start(f32[1,3,2,256,256]{4,3,2,1,0:T(8,128)} %start.1) | copy-start | bytes 4718596
  1.4 0.9 %copy-start.1 = (bf16[256,256]{1,0:T(8,128)(2,1)S(1)}, bf16[256,256]{1,0:T(8,128)(2,1)}, u32[]{:S(2)}) copy-start(bf16[256,256]{1,0:T(8,128)(2,1)} %wall.1) | copy-start | bytes 393220
  2.3 0.9 %copy-start.2 = (bf16[256,256]{1,0:T(8,128)(2,1)S(1)}, bf16[256,256]{1,0:T(8,128)(2,1)}, u32[]{:S(2)}) copy-start(bf16[256,256]{1,0:T(8,128)(2,1)} %span.1) | copy-start | bytes 393220
  3.2 0.7 %copy-start.3 = (f32[3,256]{1,0:T(4,128)S(1)}, f32[3,256]{1,0:T(4,128)}, u32[]{:S(2)}) copy-start(f32[3,256]{1,0:T(4,128)} %base.1) | copy-start | bytes 9220

commit v2 on v1

v2 whole, which is shorter than its diff:
```python
import functools

import jax
import jax.numpy as jnp
from jax import lax
from jax.experimental import pallas as pl
from jax.experimental.pallas import tpu as pltpu
from jax.sharding import PartitionSpec as P

MESH = pl.DeviceIdType.MESH
ROWS = 32
STEP = 0.2
PIECES = (1, 1, 4)


def layout(count, planes):
    if count == 2 and planes == 2:
        sends = [(0, 0, 1), (1, 1, 1)]
        return sends, 2, lambda e: e + 2 if e < 0 else e - planes
    sends = [(planes - 2, 0, 1), (planes - 1, 1, 1), (0, 2, -1), (1, 3, -1)]
    return sends, 4, lambda e: e + 2 if e < 0 else e - planes + 2


def kernel(ticks_axis, count, start, wall_hbm, span_hbm, base_hbm, out, wall, span, base, own, far, gy, gz, u1, gyr, gzr, u1r,
           rate, ub, load_sem, xs, xr, ts, tr, fs, fr):
    comps, planes, height, width = start.shape[1:]
    sends, slots, slot = layout(count, planes)
    edges = (-1, planes)
    t = lax.axis_index("tm")
    x = lax.axis_index("space")
    right, left = lax.rem(x + 1, count), lax.rem(x + count - 1, count)
    has_prev, has_next = t > 0, t < ticks_axis - 1

    loads = [pltpu.make_async_copy(src, dst, load_sem.at[i]) for i, (src, dst) in enumerate(
        ((base_hbm, base), (wall_hbm, wall), (span_hbm, span), (start.at[0], own.at[0])))]
    for load in loads:
        load.start()

    barrier = pltpu.get_barrier_semaphore()
    sides = [right] if slots == 2 else [right, left]
    for side in sides:
        pl.semaphore_signal(barrier, inc=1, device_id={"space": side}, device_id_type=MESH)

    @pl.when(has_prev)
    def _():
        pl.semaphore_signal(barrier, inc=1, device_id={"tm": t - 1}, device_id_type=MESH)

    @pl.when(has_next)
    def _():
        pl.semaphore_signal(barrier, inc=1, device_id={"tm": t + 1}, device_id_type=MESH)

    pl.semaphore_wait(barrier, len(sides) + has_prev.astype(jnp.int32) + has_next.astype(jnp.int32))

    def piece(c, j):
        rows = height // PIECES[c]
        return pl.ds(j * rows, rows)

    def across(c, i, j):
        p, k, way = sends[i]
        r = piece(c, j)
        return pltpu.make_async_remote_copy(
            src_ref=start.at[0, c, p, r], dst_ref=far.at[0, c, k, r],
            send_sem=xs.at[c, k, j], recv_sem=xr.at[c, k, j],
            device_id={"space": right if way == 1 else left}, device_id_type=MESH)

    def onward(c):
        return pltpu.make_async_remote_copy(
            src_ref=start.at[0, c], dst_ref=own.at[1, c], send_sem=ts.at[c], recv_sem=tr.at[c],
            device_id={"tm": t + 1}, device_id_type=MESH)

    def forward(c, k, j):
        r = piece(c, j)
        return pltpu.make_async_remote_copy(
            src_ref=far.at[0, c, k, r], dst_ref=far.at[1, c, k, r],
            send_sem=fs.at[c, k, j], recv_sem=fr.at[c, k, j],
            device_id={"tm": t + 1}, device_id_type=MESH)

    for c in range(comps):
        for i in range(len(sends)):
            for j in range(PIECES[c]):
                across(c, i, j).start()

    @pl.when(has_next)
    def _():
        for c in range(comps):
            onward(c).start()

    loads[0].wait()
    for c in range(comps):
        ub[c] = jnp.broadcast_to(base[c][None, :], (width, height)).T

    def grads(src, to_y, to_z):
        rounded = src[...].astype(jnp.bfloat16)
        to_y[...] = jnp.dot(wall[...], rounded, preferred_element_type=jnp.float32)
        to_z[...] = jnp.dot(rounded, span[...], preferred_element_type=jnp.float32)

    def plane(g, c, e):
        return own.at[g, c, e] if 0 <= e < planes else far.at[g, c, slot(e)]

    def after(g, c, e):
        return u1.at[g, c, e] if 0 <= e < planes else u1r.at[g, c, 0 if e < 0 else 1]

    def blocks(body):
        @pl.loop(0, height // ROWS)
        def _(b):
            body(pl.ds(pl.multiple_of(b * ROWS, ROWS), ROWS))

    def first(g):
        for c in range(comps):
            for p in range(planes):
                grads(own.at[g, c, p], gy.at[g, c, p], gz.at[g, c, p])

    def far_grads(g, c, i):
        grads(plane(g, c, edges[i]), gyr.at[g, c, i], gzr.at[g, c, i])

    def advance(g, c, p):
        def body(r):
            gx = 0.5 * (plane(g, c, p + 1)[r] - plane(g, c, p - 1)[r])
            f = -((ub[0, r] + own[g, 0, p, r]) * gx + (ub[1, r] + own[g, 1, p, r]) * gy[g, c, p, r]
                  + (ub[2, r] + own[g, 2, p, r]) * gz[g, c, p, r])
            if g == 0:
                rate[c, p, r] = f
            u1[g, c, p, r] = own[g, c, p, r] + STEP * f
        blocks(body)
        grads(u1.at[g, c, p], gy.at[g, c, p], gz.at[g, c, p])

    def far_advance(g, cs, i):
        e = edges[i]

        def body(r):
            v = [ub[d, r] + plane(g, d, e)[r] for d in range(3)]
            for c in cs:
                gx = 0.5 * (plane(g, c, e + 1)[r] - plane(g, c, e - 1)[r])
                f = -(v[0] * gx + v[1] * gyr[g, c, i, r] + v[2] * gzr[g, c, i, r])
                u1r[g, c, i, r] = plane(g, c, e)[r] + STEP * f
        blocks(body)

    def finish(g, cs, p, write):
        def body(r):
            v = [ub[d, r] + u1[g, d, p, r] for d in range(3)]
            for c in cs:
                gx = 0.5 * (after(g, c, p + 1)[r] - after(g, c, p - 1)[r])
                write(c, p, r, -(v[0] * gx + v[1] * gy[g, c, p, r] + v[2] * gz[g, c, p, r]))
        blocks(body)

    def own_part(c, p, r, f):
        rate[c, p, r] = 0.5 * STEP * (f - rate[c, p, r])

    def alone(c, p, r, f):
        out[0, c, p, r] = u1[0, c, p, r] + 0.5 * STEP * (f - rate[c, p, r])

    def joined(c, p, r, f):
        out[0, c, p, r] = u1[1, c, p, r] + STEP * f + rate[c, p, r]

    chunks = [(c, k) for c in range(comps) for _, k, _ in sends]
    foreign = lambda c, *es: {(c, slot(e)) for e in es if not 0 <= e < planes}
    needs_far = lambda c, i: set().union(
        foreign(c, edges[i] - 1, edges[i] + 1), *(foreign(d, edges[i]) for d in range(comps)))
    needs_own = lambda c, p: foreign(c, p - 1, p + 1)
    needs_end = lambda c, p: set().union(
        *(needs_own(d, p) for d in range(comps)), *(needs_own(c, q) for q in (p - 1, p + 1) if 0 <= q < planes),
        *(needs_far(c, i) for i, e in enumerate(edges) if abs(e - p) == 1))
    last = lambda needs: max([chunks.index(n) for n in needs], default=0)
    ready = lambda n, of, j: [c for c in range(comps) if last(of(c, j)) == n]

    def work(g, n, write):
        c, k = chunks[n]
        for i, e in enumerate(edges):
            if slot(e) == k:
                far_grads(g, c, i)
        for p in range(planes):
            for d in ready(n, needs_own, p):
                advance(g, d, p)
        for i in range(2):
            if ready(n, needs_far, i):
                far_advance(g, ready(n, needs_far, i), i)
        for p in range(planes):
            if ready(n, needs_end, p):
                if write is None:
                    pl.when(t == 0)(lambda: finish(g, ready(n, needs_end, p), p, alone))
                    pl.when(has_prev)(lambda: finish(g, ready(n, needs_end, p), p, own_part))
                else:
                    finish(g, ready(n, needs_end, p), p, write)

    def arrive(n):
        c, k = chunks[n]
        i = [s[1] for s in sends].index(k)
        for j in range(PIECES[c]):
            across(c, i, j).wait_recv()

            @pl.when(has_next)
            def _():
                forward(c, k, j).start()
        work(0, n, None)

    def prev_arrive(n):
        c, k = chunks[n]
        for j in range(PIECES[c]):
            forward(c, k, j).wait_recv()
        work(1, n, joined)

    for load in loads[1:]:
        load.wait()
    first(0)
    each = len(sends)
    for n in range(2 * each):
        arrive(n)

    @pl.when(has_prev)
    def _():
        for c in range(comps):
            onward(c).wait_recv()
        first(1)
        for n in range(each):
            prev_arrive(n)

    for n in range(2 * each, 3 * each - 1):
        arrive(n)

    @pl.when(has_prev)
    def _():
        for n in range(each, 3 * each - 1):
            prev_arrive(n)

    arrive(3 * each - 1)

    @pl.when(has_prev)
    def _():
        prev_arrive(3 * each - 1)

    for c in range(comps):
        for i in range(len(sends)):
            for j in range(PIECES[c]):
                across(c, i, j).wait_send()

    @pl.when(has_next)
    def _():
        for c in range(comps):
            onward(c).wait_send()
            for _, k, _ in sends:
                for j in range(PIECES[c]):
                    forward(c, k, j).wait_send()


def local(ticks_axis, count, start_states, wall_normal, spanwise, base_flow):
    _, comps, planes, height, width = start_states.shape
    slots = layout(count, planes)[1]
    vmem = lambda *shape: pltpu.VMEM(shape, jnp.float32)
    state = lambda *lead: vmem(*lead, height, width)
    return pl.pallas_call(
        functools.partial(kernel, ticks_axis, count),
        out_shape=jax.ShapeDtypeStruct(start_states.shape, jnp.float32),
        in_specs=[pl.BlockSpec(memory_space=pltpu.HBM)] * 4,
        out_specs=pl.BlockSpec(memory_space=pltpu.VMEM),
        scratch_shapes=[
            pltpu.VMEM(wall_normal.shape, wall_normal.dtype), pltpu.VMEM(spanwise.shape, spanwise.dtype),
            pltpu.VMEM(base_flow.shape, base_flow.dtype),
            state(2, comps, planes), state(2, comps, slots),
            state(2, comps, planes), state(2, comps, planes), state(2, comps, planes),
            state(2, comps, 2), state(2, comps, 2), state(2, comps, 2),
            state(comps, planes), state(3),
            pltpu.SemaphoreType.DMA((4,)),
            pltpu.SemaphoreType.DMA((comps, slots, max(PIECES))), pltpu.SemaphoreType.DMA((comps, slots, max(PIECES))),
            pltpu.SemaphoreType.DMA((comps,)), pltpu.SemaphoreType.DMA((comps,)),
            pltpu.SemaphoreType.DMA((comps, slots, max(PIECES))), pltpu.SemaphoreType.DMA((comps, slots, max(PIECES))),
        ],
        compiler_params=pltpu.CompilerParams(
            collective_id=0, has_side_effects=True, vmem_limit_bytes=63 * 1024 * 1024),
    )(start_states, wall_normal, spanwise, base_flow)


def solution(mesh):
    return jax.shard_map(
        functools.partial(local, mesh.shape["tm"], mesh.shape["space"]),
        mesh=mesh,
        in_specs=(P("tm", None, "space", None, None), P(), P(), P()),
        out_specs=P("tm", None, "space", None, None),
        check_vma=False,
    )
```

time: 50.5 us -> 48.1 us (0.952)
  local copies, waits for them, and re-layouts: 5.05 us -> 2.74 us
    unnamed x9 -> x1, local copies, waits for them, and re-layouts: 5.05 us -> 2.74 us
where the time goes in v2:
time: 48.1 us; the launch traced here: 47.9 us
  Pallas kernels  45.2 us (94%)
  local copies, waits for them, and re-layouts  2.74 us (6%)
    pallas_call x1, Pallas kernels, local(): pl.pallas_call(functools.partial(kernel, ticks_axis, count), out_shape=ja...  45.2 us
    unnamed x1, local copies, waits for them, and re-layouts  2.74 us

profile of v2, /device:TPU:24, one launch (start us, length us, event | category | flops | bytes accessed | tf_op | source)
XLA Modules:
  0.0 47.9 jit_solution(9169482059303658087)
XLA Ops:
  0.0 45.2 %shard_map.46 = f32[1,3,2,256,256]{4,3,2,1,0:T(8,128)} custom-call(f32[1,3,2,256,256]{4,3,2,1,0:T(8,128)} %start.1, bf16[256,256]{1,0:T(8,128)(2,1)} %wall_hbm.1, bf16[256,256]{1,0:T(8,128)(2,1)} %span_hbm.1, f32[3,256]{1,0:T(4,128)} %base_hbm.1), custom_call_target="tpu_custom_call" | custom-call | tf_op jit(solution)/shard_map/pallas_call | solution.py:250
  45.2 2.7 %copy.6 = f32[1,3,2,256,256]{4,3,2,1,0:T(8,128)} copy(f32[1,3,2,256,256]{4,3,2,1,0:T(8,128)} %shard_map.46) | data formatting | bytes 3145728

commit v3 on v2

--- a/solution.py
+++ b/solution.py
@@ -8,7 +8,7 @@
 from jax.sharding import PartitionSpec as P
 
 MESH = pl.DeviceIdType.MESH
-ROWS = 32
+ROWS = 64
 STEP = 0.2
 PIECES = (1, 1, 4)
 
@@ -249,7 +249,7 @@
     state = lambda *lead: vmem(*lead, height, width)
     return pl.pallas_call(
         functools.partial(kernel, ticks_axis, count),
-        out_shape=jax.ShapeDtypeStruct(start_states.shape, jnp.float32),
+        out_shape=pltpu.VMEM(start_states.shape, jnp.float32),
         in_specs=[pl.BlockSpec(memory_space=pltpu.HBM)] * 4,
         out_specs=pl.BlockSpec(memory_space=pltpu.VMEM),
         scratch_shapes=[
@@ -265,8 +265,8 @@
             pltpu.SemaphoreType.DMA((comps, slots, max(PIECES))), pltpu.SemaphoreType.DMA((comps, slots, max(PIECES))),
         ],
         compiler_params=pltpu.CompilerParams(
-            collective_id=0, has_side_effects=True, vmem_limit_bytes=63 * 1024 * 1024),
-    )(start_states, wall_normal, spanwise, base_flow)
+            collective_id=0, has_side_effects=True, vmem_limit_bytes=52 * 1024 * 1024),
+    )(*(pltpu.with_memory_space_constraint(v, pltpu.HBM) for v in (start_states, wall_normal, spanwise, base_flow)))
 
 
 def solution(mesh):

time: 48.1 us -> 44.9 us (0.933)
  Pallas kernels: 45.2 us -> 43.6 us
  local copies, waits for them, and re-layouts: 2.74 us -> 1.15 us
    pallas_call x1, Pallas kernels: 45.2 us -> 43.6 us  [local(): pl.pallas_call(functools.partial(kernel, ticks_axis, count), out_shape=pl...]
    unnamed x1, local copies, waits for them, and re-layouts: 2.74 us -> 1.15 us
where the time goes in v3:
time: 44.9 us; the launch traced here: 44.8 us
  Pallas kernels  43.6 us (97%)
  local copies, waits for them, and re-layouts  1.15 us (3%)
    pallas_call x1, Pallas kernels, local(): pl.pallas_call(functools.partial(kernel, ticks_axis, count), out_shape=pl...  43.6 us
    unnamed x1, local copies, waits for them, and re-layouts  1.15 us

profile of v3, /device:TPU:24, one launch (start us, length us, event | category | flops | bytes accessed | tf_op | source)
XLA Modules:
  0.0 44.8 jit_solution(5931959737431325682)
XLA Ops:
  0.0 43.6 %shard_map.46 = f32[1,3,2,256,256]{4,3,2,1,0:T(8,128)S(1)} custom-call(f32[1,3,2,256,256]{4,3,2,1,0:T(8,128)} %start.1, bf16[256,256]{1,0:T(8,128)(2,1)} %wall_hbm.1, bf16[256,256]{1,0:T(8,128)(2,1)} %span_hbm.1, f32[3,256]{1,0:T(4,128)} %base_hbm.1), custom_call_target="tpu_custom_call" | custom-call | tf_op jit(solution)/shard_map/pallas_call | solution.py:250
  43.6 1.1 %copy.6 = f32[1,3,2,256,256]{4,3,2,1,0:T(8,128)} copy(f32[1,3,2,256,256]{4,3,2,1,0:T(8,128)S(1)} %shard_map.46) | data formatting | bytes 3145728
